TPU v7x, 512 devices: a whole 4x4x16 slice. The times are simulated.
512 devices in a mesh: samp: 32 (over z, x_lo), par: 16 (over y, x_hi, core).
Axes of the slice: x: 4 (x_hi: 2, x_lo: 2; x = x_hi * 2 + x_lo), y: 4, z: 16, core: 2. Of those that a mesh axis runs over, the one named last changes fastest.
Arguments:
- logder: bfloat16 [16384, 16384], P('samp', 'par'), may hold values from -6 to 6
- block_of: int32 [16384], P('samp'), may hold values from 0 to 31, as said below
- plan: int32 [2, 32], replicated, may hold values from 0 to 31, as said below
Outputs:
- tiles: float32 [3, 16384, 512], P(None, ('samp', 'par'))
Inputs may be any that keep to these rules, and one draw needn't show every extreme that they name: `block_of`: among the 512 samples of each index of samp, every block is named exactly 16 times. Each row pairs the blocks: plan[r, plan[r, b]] = b and plan[r, b] != b; the two rounds share no pair (rounds of a round-robin tournament).
All inputs are finite; a program needn't handle non-finite values.
Results may differ from a plain program's by a relative error of at most 0.0003.
Values may be sent and summed in bfloat16 or wider, within the bound.
A program may use at most 64 MiB of HBM per device.

v0:
```python
import math

import jax
import jax.numpy as jnp
from jax import lax
from jax.sharding import PartitionSpec as P


def tile_of(first_rows, other_rows, scale):
    prod = lax.dot_general(
        first_rows, other_rows, (((1,), (1,)), ((), ())), preferred_element_type=jnp.float32
    )
    return prod * scale


def shards(logder, block_of, plan):
    nsamp = lax.axis_size("samp")
    npar = lax.axis_size("par")
    rows_here = logder.shape[0]
    per_block = rows_here // nsamp
    share = rows_here // npar
    scale = 1.0 / math.sqrt(logder.shape[1] * npar)
    order = jnp.argsort(block_of, stable=True).reshape(nsamp, per_block)
    own_send = logder[order.reshape(-1)]
    first_send = logder[order[plan[0]].reshape(-1)]
    second_send = logder[order[plan[1]].reshape(-1)]
    own_rows, first_rows, second_rows = (
        lax.all_to_all(own_send, "samp", split_axis=0, concat_axis=0, tiled=True),
        lax.all_to_all(first_send, "samp", split_axis=0, concat_axis=0, tiled=True),
        lax.all_to_all(second_send, "samp", split_axis=0, concat_axis=0, tiled=True),
    )
    others = (own_rows, first_rows, second_rows)
    stacked = jnp.stack([tile_of(own_rows, other, scale) for other in others])
    whole = lax.psum(stacked, "par")
    result = lax.dynamic_slice_in_dim(whole, lax.axis_index("par") * share, share, 1)
    return result


def solution(mesh):
    return jax.shard_map(
        shards,
        mesh=mesh,
        in_specs=(P("samp", "par"), P("samp"), P()),
        out_specs=P(None, ("samp", "par"), None),
        check_vma=False,
    )
```

profile of v0, /device:TPU:1, one launch (start us, length us, event | category | flops | bytes accessed | tf_op | source)
XLA Modules:
  0.0 374.5 jit_solution(18126035906289854113)
XLA Ops:
  6.5 0.0 copy-start
  6.5 0.8 fusion.3
  7.3 4.4 %sort.17 = (s32[512]{0:T(512)}, s32[512]{0:T(512)S(1)}) sort(s32[512]{0:T(512)} %param.4, s32[512]{0:T(512)S(1)} %iota.4), dimensions={0}, to_apply=%region_0.0 | sort | flops 4608 | bytes 8192 | tf_op jit(solution)/shard_map/jit(argsort)/sort | solution.py:23
  11.8 0.1 reshape.127
  11.9 0.6 gather_fusion.1
  12.4 0.1 reshape.128
  12.5 0.0 copy-done
  12.5 2.8 gather_fusion.2
  15.3 17.0 %all-to-all-start.1 = ((bf16[32,16,1024]{2,1,0:T(8,128)(2,1)}), bf16[32,16,1024]{2,1,0:T(8,128)(2,1)S(1)}, u32[]{:S(2)}, u32[]{:S(2)}) async-start(bf16[32,16,1024]{2,1,0:T(8,128)(2,1)} %bitcast.6), calls=%async_computation.1 | async-start | bytes 2097152 | tf_op jit(solution)/shard_map/all_to_all | solution.py:29
  32.3 2.8 gather_fusion
  35.1 50.3 %all-to-all-done.1 = bf16[32,16,1024]{2,1,0:T(8,128)(2,1)S(1)} async-done(((bf16[32,16,1024]{2,1,0:T(8,128)(2,1)}), bf16[32,16,1024]{2,1,0:T(8,128)(2,1)S(1)}, u32[]{:S(2)}, u32[]{:S(2)}) %all-to-all-start.1) | async-done | bytes 1048608 | tf_op jit(solution)/shard_map/all_to_all | solution.py:29
  85.4 5.5 %all-to-all-start = ((bf16[32,16,1024]{2,1,0:T(8,128)(2,1)}), bf16[32,16,1024]{2,1,0:T(8,128)(2,1)S(1)}, u32[]{:S(2)}, u32[]{:S(2)}) async-start(bf16[32,16,1024]{2,1,0:T(8,128)(2,1)} %bitcast), calls=%async_computation | async-start | bytes 2097152 | tf_op jit(solution)/shard_map/all_to_all | solution.py:28
  90.9 0.6 gather_fusion.3
  91.5 0.1 reshape.129
  91.6 2.8 gather_fusion.4
  94.4 49.7 %all-to-all-done = bf16[32,16,1024]{2,1,0:T(8,128)(2,1)S(1)} async-done(((bf16[32,16,1024]{2,1,0:T(8,128)(2,1)}), bf16[32,16,1024]{2,1,0:T(8,128)(2,1)S(1)}, u32[]{:S(2)}, u32[]{:S(2)}) %all-to-all-start) | async-done | bytes 1048608 | tf_op jit(solution)/shard_map/all_to_all | solution.py:28
  144.0 5.7 %all-to-all-start.2 = ((bf16[32,16,1024]{2,1,0:T(8,128)(2,1)}), bf16[32,16,1024]{2,1,0:T(8,128)(2,1)}, u32[]{:S(2)}, u32[]{:S(2)}) async-start(bf16[32,16,1024]{2,1,0:T(8,128)(2,1)} %bitcast.12), calls=%async_computation.2 | async-start | bytes 2097152 | tf_op jit(solution)/shard_map/all_to_all | solution.py:30
  149.7 0.0 all-reduce.2.cloned.1.call-start
  149.7 1.7 fusion.2
  151.5 1.7 fusion.1
  153.2 0.0 copy-start.1
  153.2 49.6 %all-to-all-done.2 = bf16[32,16,1024]{2,1,0:T(8,128)(2,1)} async-done(((bf16[32,16,1024]{2,1,0:T(8,128)(2,1)}), bf16[32,16,1024]{2,1,0:T(8,128)(2,1)}, u32[]{:S(2)}, u32[]{:S(2)}) %all-to-all-start.2) | async-done | bytes 1048608 | tf_op jit(solution)/shard_map/all_to_all | solution.py:30
  202.8 0.0 copy-start.2
  202.8 2.0 fusion
  204.9 0.0 copy-done.1
  204.9 0.0 copy-done.2
  204.9 2.0 pad_maximum_fusion
  206.9 0.0 all-reduce.2.cloned.1.call-update
  206.9 159.2 %all-reduce.2.cloned.1.call-done = f32[3,512,512]{2,1,0:T(8,128)} async-done(((f32[3,512,512]{2,1,0:T(8,128)}), f32[3,512,512]{2,1,0:T(8,128)}) %all-reduce.2.cloned.1.call-update) | async-done | bytes 3145744 | tf_op jit(solution)/shard_map/psum | solution.py:34
  366.1 1.6 constant_dynamic-slice_fusion
  (8 shorter events, 0.0 us)
Async XLA Ops:
  6.5 6.0 %copy-start = (bf16[512,1024]{1,0:T(8,128)(2,1)S(1)}, bf16[512,1024]{1,0:T(8,128)(2,1)}, u32[]{:S(2)}) copy-start(bf16[512,1024]{1,0:T(8,128)(2,1)} %param.3) | copy-start | bytes 3145732
  15.3 70.1 %all-to-all-start.1 = ((bf16[32,16,1024]{2,1,0:T(8,128)(2,1)}), bf16[32,16,1024]{2,1,0:T(8,128)(2,1)S(1)}, u32[]{:S(2)}, u32[]{:S(2)}) async-start(bf16[32,16,1024]{2,1,0:T(8,128)(2,1)} %bitcast.6), calls=%async_computation.1 | async-start | bytes 2097152 | tf_op jit(solution)/shard_map/all_to_all | solution.py:29
  85.4 58.6 %all-to-all-start = ((bf16[32,16,1024]{2,1,0:T(8,128)(2,1)}), bf16[32,16,1024]{2,1,0:T(8,128)(2,1)S(1)}, u32[]{:S(2)}, u32[]{:S(2)}) async-start(bf16[32,16,1024]{2,1,0:T(8,128)(2,1)} %bitcast), calls=%async_computation | async-start | bytes 2097152 | tf_op jit(solution)/shard_map/all_to_all | solution.py:28
  144.0 58.8 %all-to-all-start.2 = ((bf16[32,16,1024]{2,1,0:T(8,128)(2,1)}), bf16[32,16,1024]{2,1,0:T(8,128)(2,1)}, u32[]{:S(2)}, u32[]{:S(2)}) async-start(bf16[32,16,1024]{2,1,0:T(8,128)(2,1)} %bitcast.12), calls=%async_computation.2 | async-start | bytes 2097152 | tf_op jit(solution)/shard_map/all_to_all | solution.py:30
  149.7 216.4 %all-reduce.2.cloned.1.call-start = ((), (), s32[]{:S(2)}) async-start(), calls=%async_computation.3 | async-start | bytes 6291456 | tf_op jit(solution)/shard_map/psum | solution.py:34
  153.2 51.7 %copy-start.1 = (f32[1,512,512]{2,1,0:T(8,128)S(1)}, f32[1,512,512]{2,1,0:T(8,128)}, u32[]{:S(2)}) copy-start(f32[1,512,512]{2,1,0:T(8,128)} %fusion.2) | copy-start | bytes 3145732
  202.8 2.1 copy-start.2
Sparse Core Ops, SparseCore 0:
  207.0 158.9 all-reduce.1
where the time goes:
time: 376 us; the launch traced here: 375 us
  waiting for transfers between devices  309 us (82%)
  starting transfers between devices  28.2 us (8%)
  between operations  13.5 us (4%)
  local copies, waits for them, and re-layouts  11.3 us (3%)
  other arithmetic  7.25 us (2%)
  matrix products  5.52 us (1%)
    psum x1, waiting for transfers between devices, shards(): whole = lax.psum(stacked, 'par')  159 us
    all_to_all x1, waiting for transfers between devices, shards(): lax.all_to_all(first_send, 'samp', split_axis=0, concat_axis=0, tiled=True)  50.3 us
    all_to_all x1, waiting for transfers between devices, shards(): lax.all_to_all(own_send, 'samp', split_axis=0, concat_axis=0, tiled=True)  49.7 us
    all_to_all x1, waiting for transfers between devices, shards(): lax.all_to_all(second_send, 'samp', split_axis=0, concat_axis=0, tiled=True)  49.6 us
    all_to_all x1, starting transfers between devices, shards(): lax.all_to_all(first_send, 'samp', split_axis=0, concat_axis=0, tiled=True)  17 us
  transfers between devices with their start and end apart: 4, of which 4 were waited for; matrix products, arithmetic and copies ran while one was open for 3% of the time, Pallas kernels for 0%

commit v1 on v0

v1 whole, which is shorter than its diff:
```python
import functools
import math

import jax
import jax.numpy as jnp
from jax import lax
from jax.experimental import pallas as pl
from jax.experimental.pallas import tpu as pltpu
from jax.sharding import PartitionSpec as P

MESH = pl.DeviceIdType.MESH
NS = 32
NZ = 16
CHIPS = 8
CHIP_OFFSETS = ((0, 1), (1, 0), (3, 0), (1, 1), (3, 1), (2, 0), (2, 1))


def layout_kernel(plan, block_of, place, table, seen):
    def clear(b, carry):
        seen[b] = 0
        return carry

    lax.fori_loop(0, NS, clear, 0)

    def cycle(first, base):
        def walk():
            def more(state):
                return (state[0] != first) & (state[1] < NZ)

            def step(state):
                return plan[1, plan[0, state[0]]], state[1] + 1

            _, m = lax.while_loop(more, step, (plan[1, plan[0, first]], jnp.int32(1)))

            def put(b, k, after, before):
                seen[b] = 1
                out = k < m
                t = jnp.where(out, 2 * (base + k), 2 * (base + 2 * m - 1 - k) + 1)
                nxt = jnp.where(out, jnp.where(k == m - 1, 2, 0), jnp.where(k == 2 * m - 1, 2, 1))
                prv = jnp.where(out, jnp.where(k == 0, 2, 1), jnp.where(k == m, 2, 0))
                table[0, b] = t
                table[after, t] = nxt
                table[before, t] = prv

            def pair(i, u):
                v = plan[0, u]
                put(u, 2 * i, 1, 2)
                put(v, 2 * i + 1, 2, 1)
                return plan[1, v]

            lax.fori_loop(0, m, pair, first)
            return base + m

        return lax.cond(seen[first] == 0, walk, lambda: base)

    lax.fori_loop(0, NS, cycle, jnp.int32(0))

    rows = block_of.shape[1]
    block_at = lax.broadcasted_iota(jnp.int32, (NS, rows), 0)
    mine = block_at == block_of[...]
    earlier = lax.broadcasted_iota(jnp.int32, (rows, rows), 0) < lax.broadcasted_iota(jnp.int32, (rows, rows), 1)
    rank = jnp.dot(mine.astype(jnp.bfloat16), earlier.astype(jnp.bfloat16), preferred_element_type=jnp.float32)
    start = jnp.zeros((NS, rows), jnp.int32)
    for b in range(NS):
        start = jnp.where(block_at == b, table[0, b] * (rows // NS), start)
    spot = jnp.where(mine, rank.astype(jnp.int32) + start, 0)
    place[...] = jnp.sum(spot, axis=0, keepdims=True)


def main_kernel(
    scale,
    table,
    place,
    logder,
    out,
    sorted_rows,
    own,
    near,
    own_part,
    own_pair,
    own_share,
    own_in,
    edge_part,
    edge_pair,
    edge_share,
    edge_in,
    own_piece,
    own_mid,
    own_turn,
    own_home,
    edge_piece,
    edge_mid,
    edge_turn,
    edge_home,
    send,
    rows_recv,
    near_recv,
    pair_recv,
    own_chip_recv,
    edge_chip_recv,
    mid_recv,
    home_recv,
):
    me = lax.axis_index("samp")
    par = lax.axis_index("par")
    z, x = me // 2, me % 2
    chip, core = par // 2, par % 2
    y, x_hi = chip // 2, chip % 2
    rows = logder.shape[0]
    per = rows // NS
    share = rows // (2 * CHIPS)

    def ring(k):
        return jnp.where(k % 2 == 1, (k + 1) // 2, NS - k // 2)

    def to_samp(s):
        return {"samp": s}

    def chip_at(offset):
        return lax.rem(y + offset[0], 4) * 2 + lax.rem(x_hi + offset[1], 2)

    def remote(src, dst, send_sem, recv_sem, device):
        return pltpu.make_async_remote_copy(
            src_ref=src, dst_ref=dst, send_sem=send_sem, recv_sem=recv_sem, device_id=device, device_id_type=MESH
        )

    def await_bytes(ref, sem):
        pltpu.make_async_copy(ref, ref, sem).wait()

    barrier = pltpu.get_barrier_semaphore()

    def greet(k, carry):
        pl.semaphore_signal(barrier, inc=1, device_id=to_samp(lax.rem(me + k, NS)), device_id_type=MESH)
        return carry

    lax.fori_loop(1, NS, greet, 0)
    pl.semaphore_signal(barrier, inc=1, device_id={"par": chip * 2 + 1 - core}, device_id_type=MESH)
    for offset in CHIP_OFFSETS:
        pl.semaphore_signal(barrier, inc=1, device_id={"par": chip_at(offset) * 2 + core}, device_id_type=MESH)

    pick = (lax.broadcasted_iota(jnp.int32, (rows, rows), 0) == place[...]).astype(jnp.bfloat16)
    sorted_rows[...] = jnp.dot(pick, logder[...], preferred_element_type=jnp.float32).astype(jnp.bfloat16)
    pl.semaphore_wait(barrier, NS - 1 + 1 + len(CHIP_OFFSETS))

    def chunk(s):
        return pl.ds(pl.multiple_of(s * per, per), per)

    def send_rows(k, carry):
        to = lax.rem(me + ring(k), NS)
        remote(sorted_rows.at[chunk(to)], own.at[chunk(me)], send.at[0], rows_recv.at[k], to_samp(to)).start()
        return carry

    lax.fori_loop(1, NS, send_rows, 0)
    own[chunk(me), :] = sorted_rows[chunk(me), :]

    above = lax.rem(z + 1, NZ) * 2 + x
    below = lax.rem(z + NZ - 1, NZ) * 2 + x
    across = z * 2 + 1 - x

    def pass_on(s):
        for slot, to in ((1, above), (0, below), (2, across)):
            remote(own.at[chunk(s)], near.at[slot, chunk(s)], send.at[1], near_recv.at[slot], to_samp(to)).start()

    pass_on(me)

    def arrive(k, carry):
        s = lax.rem(me + NS - ring(k), NS)
        await_bytes(own.at[chunk(s)], rows_recv.at[k])
        pass_on(s)
        return carry

    lax.fori_loop(1, NS, arrive, 0)

    def tile_of(other):
        return lax.dot_general(own[...], other, (((1,), (1,)), ((), ())), preferred_element_type=jnp.float32)

    def to_pair(part, pair, n):
        copy = remote(part.at[1 - core], pair, send.at[2 + n], pair_recv.at[n], {"par": chip * 2 + 1 - core})
        copy.start()
        return copy

    def to_chips(held, landing, sem, n):
        copies = []
        for i, offset in enumerate(CHIP_OFFSETS):
            to = chip_at(offset)
            copy = remote(held.at[to], landing.at[i], send.at[4 + n], sem.at[i], {"par": to * 2 + core})
            copy.start()
            copies.append(copy)
        return copies

    def exchange(piece, landing, sem, n):
        def one(k, carry):
            to = lax.rem(me + ring(k), NS)
            remote(piece.at[to], landing.at[me], send.at[n], sem, to_samp(to)).start()
            return carry

        lax.fori_loop(1, NS, one, 0)
        landing[me] = piece[me]

    def await_exchange(landing, sem):
        await_bytes(landing.at[pl.ds(0, NS - 1)], sem)

    def turn(mid, turned):
        for b in range(NS):
            turned[b] = mid[table[0, b]]

    product = tile_of(own[...])
    for c in range(2):
        for j in range(CHIPS):
            at = (2 * j + c) * share
            own_part[c, j] = product[at : at + share]
    to_pair(own_part, own_pair, 0).wait_recv()
    own_share[...] = own_part[core] + own_pair[...]
    copies = to_chips(own_share, own_in, own_chip_recv, 0)
    total = own_share[chip]
    for i, copy in enumerate(copies):
        copy.wait_recv()
        total += own_in[i]
    total *= scale
    for i in range(NS):
        a, l = (i // 4) * (share // 8), (i % 4) * 128
        own_piece[i] = total[a : a + share // 8, l : l + 128]
    exchange(own_piece, own_mid, mid_recv.at[0], 6)

    for slot in range(3):
        await_bytes(near.at[slot], near_recv.at[slot])
    for r in range(2):
        product = tile_of(near[table[1 + r, me]])
        for c in range(2):
            for j in range(CHIPS):
                at = (2 * j + c) * share
                edge_part[c, j, r] = product[at : at + share]
    to_pair(edge_part, edge_pair, 1).wait_recv()
    edge_share[...] = edge_part[core] + edge_pair[...]
    copies = to_chips(edge_share, edge_in, edge_chip_recv, 1)

    await_exchange(own_mid, mid_recv.at[0])
    turn(own_mid, own_turn)
    exchange(own_turn, own_home, home_recv.at[0], 7)

    total = edge_share[chip]
    for i, copy in enumerate(copies):
        copy.wait_recv()
        total += edge_in[i]
    total *= scale
    for i in range(NS):
        a, l = ((i % 16) // 4) * (share // 4), (i % 4) * 128
        edge_piece[i] = total[i // 16, a : a + share // 4, l : l + 128]
    exchange(edge_piece, edge_mid, mid_recv.at[1], 8)

    await_exchange(own_home, home_recv.at[0])
    for i in range(NS):
        a, l = (i // 4) * (share // 8), (i % 4) * 128
        out[0, a : a + share // 8, l : l + 128] = own_home[i]

    await_exchange(edge_mid, mid_recv.at[1])
    turn(edge_mid, edge_turn)
    exchange(edge_turn, edge_home, home_recv.at[1], 9)
    await_exchange(edge_home, home_recv.at[1])
    for i in range(NS):
        a, l = ((i % 16) // 4) * (share // 4), (i % 4) * 128
        out[1 + i // 16, a : a + share // 4, l : l + 128] = edge_home[i]

    await_bytes(own.at[pl.ds(0, rows - per)], send.at[0])
    await_bytes(near, send.at[1])
    await_bytes(own_pair, send.at[2])
    await_bytes(edge_pair, send.at[3])
    await_bytes(own_in, send.at[4])
    await_bytes(edge_in, send.at[5])
    for n, piece in ((6, own_piece), (7, own_turn), (8, edge_piece), (9, edge_turn)):
        await_exchange(piece, send.at[n])


def shards(logder, block_of, plan):
    rows, columns = logder.shape
    share = rows // (2 * CHIPS)
    smem = pl.BlockSpec(memory_space=pltpu.SMEM)
    vmem = pl.BlockSpec(memory_space=pltpu.VMEM)
    place, table = pl.pallas_call(
        layout_kernel,
        name="layout",
        out_shape=(jax.ShapeDtypeStruct((1, rows), jnp.int32), jax.ShapeDtypeStruct((3, NS), jnp.int32)),
        in_specs=[smem, vmem],
        out_specs=(vmem, smem),
        scratch_shapes=[pltpu.SMEM((NS,), jnp.int32)],
    )(plan, block_of.reshape(1, rows))
    scale = 1.0 / math.sqrt(columns * lax.axis_size("par"))
    f32, bf16 = jnp.float32, jnp.bfloat16
    own_pieces = pltpu.VMEM((NS, share // 8, 128), f32)
    edge_pieces = pltpu.VMEM((NS, share // 4, 128), f32)
    return pl.pallas_call(
        functools.partial(main_kernel, scale),
        name="tiles",
        out_shape=jax.ShapeDtypeStruct((3, share, rows), f32),
        in_specs=[smem, vmem, vmem],
        out_specs=vmem,
        scratch_shapes=[
            pltpu.VMEM((rows, columns), bf16),
            pltpu.VMEM((rows, columns), bf16),
            pltpu.VMEM((3, rows, columns), bf16),
            pltpu.VMEM((2, CHIPS, share, rows), f32),
            pltpu.VMEM((CHIPS, share, rows), f32),
            pltpu.VMEM((CHIPS, share, rows), f32),
            pltpu.VMEM((CHIPS - 1, share, rows), f32),
            pltpu.VMEM((2, CHIPS, 2, share, rows), f32),
            pltpu.VMEM((CHIPS, 2, share, rows), f32),
            pltpu.VMEM((CHIPS, 2, share, rows), f32),
            pltpu.VMEM((CHIPS - 1, 2, share, rows), f32),
            own_pieces,
            own_pieces,
            own_pieces,
            own_pieces,
            edge_pieces,
            edge_pieces,
            edge_pieces,
            edge_pieces,
            pltpu.SemaphoreType.DMA((10,)),
            pltpu.SemaphoreType.DMA((NS,)),
            pltpu.SemaphoreType.DMA((3,)),
            pltpu.SemaphoreType.DMA((2,)),
            pltpu.SemaphoreType.DMA((CHIPS - 1,)),
            pltpu.SemaphoreType.DMA((CHIPS - 1,)),
            pltpu.SemaphoreType.DMA((2,)),
            pltpu.SemaphoreType.DMA((2,)),
        ],
        compiler_params=pltpu.CompilerParams(
            collective_id=0, has_side_effects=True, vmem_limit_bytes=48 * 1024 * 1024
        ),
    )(table, place, logder)


def solution(mesh):
    return jax.shard_map(
        shards,
        mesh=mesh,
        in_specs=(P("samp", "par"), P("samp"), P()),
        out_specs=P(None, ("samp", "par"), None),
        check_vma=False,
    )
```

time: 376 us -> 133 us (0.35)
  waiting for transfers between devices: 309 us -> 0 us
  Pallas kernels: 0 us -> 129 us
  starting transfers between devices: 28.2 us -> 0 us
  between operations: 13.5 us -> 0.03 us
  local copies, waits for them, and re-layouts: 11.3 us -> 3.24 us
  other arithmetic: 7.25 us -> 0 us
  matrix products: 5.52 us -> 0 us
    psum x1 -> x0, waiting for transfers between devices: 159 us -> none  [shards(): whole = lax.psum(stacked, 'par')]
    all_to_all x3 -> x0, waiting for transfers between devices: 150 us -> none  [the longest x1 50.3 us: shards(): lax.all_to_all(first_send, 'samp', split_axis=0, concat_axis=0, tiled=True)]
    pallas_call x0 -> x2, Pallas kernels: none -> 129 us  [the longest x1 127 us: shards(): pl.pallas_call(functools.partial(main_kernel, scale), name='tiles', out_s...]
    all_to_all x3 -> x0, starting transfers between devices: 28.1 us -> none  [the longest x1 17 us: shards(): lax.all_to_all(first_send, 'samp', split_axis=0, concat_axis=0, tiled=True)]
    gather x5 -> x0, local copies, waits for them, and re-layouts: 9.45 us -> none  [the longest x2 3.34 us: shards(): first_send = logder[order[plan[0]].reshape(-1)]]
    dot_general x3 -> x0, matrix products: 5.52 us -> none  [tile_of(): lax.dot_general(first_rows, other_rows, (((1,), (1,)), ((), ())), preferr...]
    sort x1 -> x0, other arithmetic: 4.45 us -> none  [shards(): order = jnp.argsort(block_of, stable=True).reshape(nsamp, per_block)]
  transfers between devices with their start and end apart: 4 -> 0, of which waited for: 4 -> 0; matrix products, arithmetic and copies ran while one was open for 3% -> 0% of each run, Pallas kernels for 0% -> 0%
where the time goes in v1:
time: 133 us
  Pallas kernels  129 us (97%)
  local copies, waits for them, and re-layouts  3.24 us (2%)
    pallas_call x1, Pallas kernels, shards(): pl.pallas_call(functools.partial(main_kernel, scale), name='tiles', out_s...  127 us
    unnamed x7, local copies, waits for them, and re-layouts  3.24 us
    pallas_call x1, Pallas kernels, shards(): pl.pallas_call(layout_kernel, name='layout', out_shape=(jax.ShapeDtypeStr...  2.77 us

profile of v1, /device:TPU:1, one launch (start us, length us, event | category | flops | bytes accessed | tf_op | source)
XLA Modules:
  0.0 132.7 jit_solution(1426726745394004242)
XLA Ops:
  0.0 2.8 %layout.1 = (s32[1,512]{1,0:T(1,128)}, s32[3,32]{1,0:T(4,128)}) custom-call(s32[2,32]{1,0:T(2,128)} %plan.1, s32[1,512]{1,0:T(1,128)} %bitcast.1), custom_call_target="tpu_custom_call" | custom-call | tf_op jit(solution)/shard_map/layout/pallas_call | solution.py:279
  2.8 0.0 copy-start.1
  2.8 0.7 copy-done.1
  3.5 0.0 copy-start
  3.5 1.2 copy-done
  4.7 0.0 copy-start.2
  4.7 0.7 copy-done.2
  5.3 126.7 %tiles.1 = f32[3,32,512]{2,1,0:T(8,128)S(1)} custom-call(s32[3,32]{1,0:T(4,128)S(1)} %copy-done.2, s32[1,512]{1,0:T(1,128)S(1)} %copy-done.1, bf16[512,1024]{1,0:T(8,128)(2,1)S(1)} %copy-done), custom_call_target="tpu_custom_call" | custom-call | tf_op jit(solution)/shard_map/tiles/pallas_call | solution.py:291
  132.1 0.7 copy.5
Async XLA Ops:
  2.8 0.7 copy-start.1
  3.5 1.2 copy-start
  4.7 0.7 copy-start.2

commit v2 on v0

v2 whole, which is shorter than its diff:
```python
import functools
import math

import jax
import jax.numpy as jnp
from jax import lax
from jax.experimental import pallas as pl
from jax.experimental.pallas import tpu as pltpu
from jax.sharding import PartitionSpec as P

MESH = pl.DeviceIdType.MESH
NS = 32
NZ = 16
CHIPS = 8
NY = 4
GROUPS = ((0, 256), (256, 128), (384, 128))
STEPS = 16
WINDOW = 5
BITS = (-0x55555556, -0x33333334, -0x0F0F0F10, -0x00FF0100, -0x00010000)


def ladder(plan):
    block = first = k = seen = jnp.int32(0)
    walk = []
    for j in range(NS):
        seen = seen | lax.shift_left(jnp.int32(1), block)
        after = plan[j % 2, block]
        closed = None
        if j % 2 == 1:
            closed = after == first
        walk.append((block, k, closed))
        if closed is None:
            block, k = after, k + 1
        else:
            free = ~seen & (seen + 1)
            lowest = jnp.int32(0)
            for i, bits in enumerate(BITS):
                lowest = lowest + jnp.where((free & bits) != 0, 1 << i, 0)
            first = jnp.where(closed, lowest, first)
            block = jnp.where(closed, lowest, after)
            k = jnp.where(closed, 0, k + 1)
    steps = []
    length = jnp.int32(0)
    for j in reversed(range(NS)):
        block, k, closed = walk[j]
        if closed is not None:
            length = jnp.where(closed, k + 1, length)
        m = lax.shift_right_logical(length, 1)
        out = k < m
        position = jnp.where(out, j + k, j - 3 * k + 2 * length - 1)
        onward = jnp.where(out, jnp.where(k == m - 1, 2, 0), jnp.where(k == length - 1, 2, 1))
        back = jnp.where(out, jnp.where(k == 0, 2, 1), jnp.where(k == m, 2, 0))
        steps.append((block, position, (onward, back) if j % 2 == 0 else (back, onward)))
    return steps


def tiles_kernel(scale, logder, block_of, plan, out, *scratch):
    (
        raw, blocks, pairs, place, table, sorted_rows, own, near, parts, pair_in, shares, y_in, halves, x_in,
        piece, mid, turned, home, local, send, rows_send, rows_recv, near_send, near_recv, pair_recv, y_recv, x_recv, mid_recv, home_recv,
    ) = scratch
    me = lax.axis_index("samp")
    par = lax.axis_index("par")
    z, x = me // 2, me % 2
    chip, core = par // 2, par % 2
    y, x_hi = chip // 2, chip % 2
    rows = raw.shape[0]
    per = rows // NS
    share = rows // (2 * CHIPS)
    units = len(parts)

    def ring(k):
        return jnp.where(k % 2 == 1, (k + 1) // 2, NS - k // 2)

    def along_y(d):
        return {"par": (lax.rem(y + d, NY) * 2 + x_hi) * 2 + core}

    other_core = {"par": chip * 2 + 1 - core}
    other_x = {"par": (y * 2 + 1 - x_hi) * 2 + core}

    def remote(src, dst, send_sem, recv_sem, device):
        return pltpu.make_async_remote_copy(
            src_ref=src, dst_ref=dst, send_sem=send_sem, recv_sem=recv_sem, device_id=device, device_id_type=MESH
        )

    def await_bytes(ref, sem):
        pltpu.make_async_copy(ref, ref, sem).wait()

    arrivals = [
        pltpu.make_async_copy(plan, pairs, local.at[0]),
        pltpu.make_async_copy(block_of, blocks, local.at[1]),
        pltpu.make_async_copy(logder, raw, local.at[2]),
    ]
    for copy in arrivals:
        copy.start()

    barrier = pltpu.get_barrier_semaphore()

    def greet(k, carry):
        pl.semaphore_signal(barrier, inc=1, device_id={"samp": lax.rem(me + k, NS)}, device_id_type=MESH)
        return carry

    lax.fori_loop(1, NS, greet, 0)
    in_plane = [other_core, other_x] + [along_y(d) for d in range(1, NY)]
    for device in in_plane:
        pl.semaphore_signal(barrier, inc=1, device_id=device, device_id_type=MESH)

    arrivals[0].wait()
    steps = ladder(pairs)
    arrivals[1].wait()
    block_at = lax.broadcasted_iota(jnp.int32, (NS, rows), 0)
    mine = block_at == blocks[...]
    earlier = lax.broadcasted_iota(jnp.int32, (rows, rows), 0) < lax.broadcasted_iota(jnp.int32, (rows, rows), 1)
    rank = jnp.dot(mine.astype(jnp.bfloat16), earlier.astype(jnp.bfloat16), preferred_element_type=jnp.float32)
    lane = lax.broadcasted_iota(jnp.int32, place.shape, 1)
    start = jnp.zeros((NS, rows), jnp.int32)
    placed = jnp.zeros(place.shape, jnp.int32)
    sides = [jnp.int32(0), jnp.int32(0)]
    for block, position, where in steps:
        start = jnp.where(block_at == block, position * per, start)
        placed = jnp.where(lane == block, position, placed)
        for r in range(2):
            sides[r] = jnp.where(position == me, where[r], sides[r])
    place[...] = placed
    to_table = pltpu.make_async_copy(place, table, local.at[3])
    to_table.start()
    spot = jnp.where(mine, rank.astype(jnp.int32) + start, 0)
    spot = jnp.sum(spot, axis=0, keepdims=True)
    pick = (lax.broadcasted_iota(jnp.int32, (rows, rows), 0) == spot).astype(jnp.bfloat16)
    arrivals[2].wait()
    sorted_rows[...] = jnp.dot(pick, raw[...], preferred_element_type=jnp.float32).astype(jnp.bfloat16)
    pl.semaphore_wait(barrier, NS - 1 + len(in_plane))

    def chunk(s):
        return pl.ds(pl.multiple_of(s * per, per), per)

    def send_rows(k, carry):
        to = lax.rem(me + ring(NS - k), NS)
        remote(sorted_rows.at[chunk(to)], own.at[chunk(me)], rows_send, rows_recv.at[NS - k], {"samp": to}).start()
        return carry

    lax.fori_loop(1, NS, send_rows, 0)
    own[chunk(me), :] = sorted_rows[chunk(me), :]
    to_table.wait()

    def arrive(k, carry):
        s = lax.rem(me + NS - ring(k), NS)
        await_bytes(own.at[chunk(s)], rows_recv.at[k])
        return carry

    lax.fori_loop(1, NS, arrive, 0)

    above = lax.rem(z + 1, NZ) * 2 + x
    below = lax.rem(z + NZ - 1, NZ) * 2 + x
    across = z * 2 + 1 - x
    step_rows = rows // STEPS
    handed = [0]

    def hand_on(upto):
        for i in range(handed[0], upto):
            if i >= WINDOW:
                await_bytes(near[0].at[:, pl.ds(0, step_rows)], near_send.at[i - WINDOW])
            part = pl.ds(i * step_rows, step_rows)
            g = sum(i * step_rows >= first for first, _ in GROUPS) - 1
            there = pl.ds(i * step_rows - GROUPS[g][0], step_rows)
            for slot, to in ((1, above), (0, below), (2, across)):
                landing = near[g].at[slot, there]
                remote(own.at[part], landing, near_send.at[i], near_recv.at[g, slot], {"samp": to}).start()
        handed[0] = max(handed[0], upto)

    def multiply(other):
        return lax.dot_general(own[...], other, (((1,), (1,)), ((), ())), preferred_element_type=jnp.float32)

    def to_pair(u):
        remote(parts[u].at[1 - core], pair_in[u], send.at[u], pair_recv.at[u], other_core).start()

    def to_ys(u):
        await_bytes(pair_in[u], pair_recv.at[u])
        shares[u][...] = parts[u][core] + pair_in[u][...]
        for d in (1, 3, 2):
            to = pl.ds(2 * lax.rem(y + d, NY), 2)
            remote(shares[u].at[to], y_in[u].at[d - 1], send.at[units + u], y_recv.at[u, d - 1], along_y(d)).start()

    def to_x(u):
        total = shares[u][pl.ds(2 * y, 2)]
        for i in range(NY - 1):
            await_bytes(y_in[u].at[i], y_recv.at[u, i])
            total += y_in[u][i]
        halves[u][...] = total
        remote(halves[u].at[1 - x_hi], x_in[u], send.at[2 * units + u], x_recv.at[u], other_x).start()

    def whole(u):
        await_bytes(x_in[u], x_recv.at[u])
        return (halves[u][x_hi] + x_in[u][...]) * scale

    def own_tile(u):
        product = multiply(own[...])
        for c in range(2):
            for j in range(CHIPS):
                at = (2 * j + c) * share
                parts[u][c, j] = product[at : at + share]
        to_pair(u)

    def partner_tiles(u, g):
        for slot in range(3):
            await_bytes(near[g].at[slot], near_recv.at[g, slot])
        for r in range(2):
            product = multiply(near[g][sides[r]])
            for c in range(2):
                for j in range(CHIPS):
                    at = (2 * j + c) * share
                    parts[u][c, j, r] = product[at : at + share]
        to_pair(u)

    def exchange(src, landing, sem, recv_sem):
        def one(k, carry):
            to = lax.rem(me + ring(NS - k), NS)
            remote(src.at[to], landing.at[me], sem, recv_sem, {"samp": to}).start()
            return carry

        lax.fori_loop(1, NS, one, 0)
        landing[me] = src[me]

    def await_exchange(ref, sem):
        await_bytes(ref.at[pl.ds(0, NS - 1)], sem)

    sent_mid, sent_home = 3 * units, 3 * units + 2

    def to_mid(n):
        exchange(piece[n], mid[n], send.at[sent_mid + n], mid_recv.at[n])

    def to_home(n):
        await_exchange(mid[n], mid_recv.at[n])
        for b in range(NS):
            turned[n][b] = mid[n][table[0, b]]
        exchange(turned[n], home[n], send.at[sent_home + n], home_recv.at[n])

    def own_pieces():
        total = whole(0)
        for i in range(16):
            a, l = 8 * (i // 4), 128 * (i % 4)
            piece[0][i] = total[a : a + 8, l : l + 128]

    def first_pieces():
        total = whole(1)
        for i in range(16):
            r, a, l = i // 8, 8 * (i % 8 // 2), 128 * (i % 2)
            piece[0][16 + i] = total[r, a : a + 8, l : l + 128]

    def later_pieces(h):
        total = whole(2 + h)
        for i in range(16):
            r, a = i // 8, 4 * (i % 8)
            piece[1][16 * h + i] = total[r, a : a + 4]

    hand_on(WINDOW)
    own_tile(0)
    hand_on(WINDOW + 2)
    to_ys(0)
    hand_on(12)
    to_x(0)
    hand_on(13)
    partner_tiles(1, 0)
    hand_on(14)
    to_ys(1)
    hand_on(STEPS)
    own_pieces()
    partner_tiles(2, 1)
    to_ys(2)
    to_x(1)
    partner_tiles(3, 2)
    to_x(2)
    to_ys(3)
    first_pieces()
    to_mid(0)
    later_pieces(0)
    to_x(3)
    later_pieces(1)
    to_mid(1)
    to_home(0)
    to_home(1)
    await_exchange(home[0], home_recv.at[0])
    for i in range(16):
        a, l = 8 * (i // 4), 128 * (i % 4)
        out[0, a : a + 8, l : l + 128] = home[0][i]
        r, a, l = i // 8, 8 * (i % 8 // 2), 128 * (i % 2)
        out[1 + r, a : a + 8, l : l + 128] = home[0][16 + i]
    await_exchange(home[1], home_recv.at[1])
    for i in range(NS):
        h, r, a = i // 16, i % 16 // 8, 4 * (i % 8)
        out[1 + r, a : a + 4, 256 + 128 * h : 384 + 128 * h] = home[1][i]

    await_bytes(own.at[pl.ds(0, rows - per)], rows_send)
    for i in range(STEPS - WINDOW, STEPS):
        await_bytes(near[0].at[:, pl.ds(0, step_rows)], near_send.at[i])
    for u in range(units):
        await_bytes(pair_in[u], send.at[u])
        await_bytes(y_in[u], send.at[units + u])
        await_bytes(x_in[u], send.at[2 * units + u])
    for n in range(2):
        await_exchange(piece[n], send.at[sent_mid + n])
        await_exchange(turned[n], send.at[sent_home + n])


def shards(logder, block_of, plan):
    rows, columns = logder.shape
    share = rows // (2 * CHIPS)
    anywhere = pl.BlockSpec(memory_space=pl.ANY)
    scale = 1.0 / math.sqrt(columns * lax.axis_size("par"))
    f32, bf16, i32 = jnp.float32, jnp.bfloat16, jnp.int32
    kinds = ((share, rows),) + tuple((2, share, count) for _, count in GROUPS)
    sizes = (8, 4)

    def buffers(*lead):
        return [pltpu.VMEM(lead + kind, f32) for kind in kinds]

    def pieces():
        return [pltpu.VMEM((NS, size, 128), f32) for size in sizes]

    sems = pltpu.SemaphoreType.DMA
    units = len(kinds)
    return pl.pallas_call(
        functools.partial(tiles_kernel, scale),
        name="tiles",
        out_shape=jax.ShapeDtypeStruct((3, share, rows), f32),
        in_specs=[anywhere, anywhere, anywhere],
        out_specs=pl.BlockSpec(memory_space=pltpu.VMEM),
        scratch_shapes=[
            pltpu.VMEM((rows, columns), bf16),
            pltpu.VMEM((1, rows), i32),
            pltpu.SMEM((2, NS), i32),
            pltpu.VMEM((8, 128), i32),
            pltpu.SMEM((8, 128), i32),
            pltpu.VMEM((rows, columns), bf16),
            pltpu.VMEM((rows, columns), bf16),
            [pltpu.VMEM((3, count, columns), bf16) for _, count in GROUPS],
            buffers(2, CHIPS),
            buffers(CHIPS),
            buffers(CHIPS),
            buffers(NY - 1, 2),
            buffers(2),
            buffers(),
            pieces(),
            pieces(),
            pieces(),
            pieces(),
            sems((4,)),
            sems((3 * units + 2 * len(sizes),)),
            sems,
            sems((NS,)),
            sems((STEPS,)),
            sems((len(GROUPS), 3)),
            sems((units,)),
            sems((units, NY - 1)),
            sems((units,)),
            sems((len(sizes),)),
            sems((len(sizes),)),
        ],
        compiler_params=pltpu.CompilerParams(
            collective_id=0, has_side_effects=True, vmem_limit_bytes=62 * 1024 * 1024
        ),
    )(logder, block_of.reshape(1, rows), plan)


def solution(mesh):
    return jax.shard_map(
        shards,
        mesh=mesh,
        in_specs=(P("samp", "par"), P("samp"), P()),
        out_specs=P(None, ("samp", "par"), None),
        check_vma=False,
    )
```

time: 376 us -> 120 us (0.32)
  waiting for transfers between devices: 309 us -> 0 us
  Pallas kernels: 0 us -> 118 us
  starting transfers between devices: 28.2 us -> 0 us
  between operations: 13.5 us -> 0.01 us
  local copies, waits for them, and re-layouts: 11.3 us -> 1.62 us
  other arithmetic: 7.25 us -> 0 us
  matrix products: 5.52 us -> 0 us
    psum x1 -> x0, waiting for transfers between devices: 159 us -> none  [shards(): whole = lax.psum(stacked, 'par')]
    all_to_all x3 -> x0, waiting for transfers between devices: 150 us -> none  [the longest x1 50.3 us: shards(): lax.all_to_all(first_send, 'samp', split_axis=0, concat_axis=0, tiled=True)]
    pallas_call x0 -> x1, Pallas kernels: none -> 118 us  [shards(): pl.pallas_call(functools.partial(tiles_kernel, scale), name='tiles', out_...]
    all_to_all x3 -> x0, starting transfers between devices: 28.1 us -> none  [the longest x1 17 us: shards(): lax.all_to_all(first_send, 'samp', split_axis=0, concat_axis=0, tiled=True)]
    gather x5 -> x0, local copies, waits for them, and re-layouts: 9.45 us -> none  [the longest x2 3.34 us: shards(): first_send = logder[order[plan[0]].reshape(-1)]]
    dot_general x3 -> x0, matrix products: 5.52 us -> none  [tile_of(): lax.dot_general(first_rows, other_rows, (((1,), (1,)), ((), ())), preferr...]
    sort x1 -> x0, other arithmetic: 4.45 us -> none  [shards(): order = jnp.argsort(block_of, stable=True).reshape(nsamp, per_block)]
  transfers between devices with their start and end apart: 4 -> 0, of which waited for: 4 -> 0; matrix products, arithmetic and copies ran while one was open for 3% -> 0% of each run, Pallas kernels for 0% -> 0%
where the time goes in v2:
time: 120 us
  Pallas kernels  118 us (98%)
  local copies, waits for them, and re-layouts  1.62 us (1%)
    pallas_call x1, Pallas kernels, shards(): pl.pallas_call(functools.partial(tiles_kernel, scale), name='tiles', out_...  118 us

profile of v2, /device:TPU:1, one launch (start us, length us, event | category | flops | bytes accessed | tf_op | source)
XLA Modules:
  0.0 119.7 jit_solution(15058806772361486492)
XLA Ops:
  0.0 118.1 %tiles.1 = f32[3,32,512]{2,1,0:T(8,128)} custom-call(bf16[512,1024]{1,0:T(8,128)(2,1)} %logder.1, s32[1,512]{1,0:T(1,128)} %bitcast.1, s32[2,32]{1,0:T(2,128)} %plan.1), custom_call_target="tpu_custom_call" | custom-call | tf_op jit(solution)/shard_map/tiles/pallas_call | solution.py:322
  118.1 1.6 %copy.5 = f32[3,32,512]{2,1,0:T(8,128)} copy(f32[3,32,512]{2,1,0:T(8,128)} %tiles.1) | data formatting | bytes 393216

commit v3 on v2

--- a/solution.py
+++ b/solution.py
@@ -13,9 +13,12 @@
 NZ = 16
 CHIPS = 8
 NY = 4
+CHIP_OFFSETS = ((2, 1), (1, 1), (3, 1), (0, 1), (2, 0), (1, 0), (3, 0))
 GROUPS = ((0, 256), (256, 128), (384, 128))
 STEPS = 16
-WINDOW = 5
+WINDOW = 8
+DIRECT = (3,)
+EARLY = 2
 BITS = (-0x55555556, -0x33333334, -0x0F0F0F10, -0x00FF0100, -0x00010000)
 
 
@@ -57,7 +60,7 @@
 def tiles_kernel(scale, logder, block_of, plan, out, *scratch):
     (
         raw, blocks, pairs, place, table, sorted_rows, own, near, parts, pair_in, shares, y_in, halves, x_in,
-        piece, mid, turned, home, local, send, rows_send, rows_recv, near_send, near_recv, pair_recv, y_recv, x_recv, mid_recv, home_recv,
+        piece, mid, turned, home, local, send, rows_send, rows_recv, near_send, near_recv, pair_recv, y_recv, x_recv, chip_recv, mid_recv, home_recv,
     ) = scratch
     me = lax.axis_index("samp")
     par = lax.axis_index("par")
@@ -75,6 +78,12 @@
     def along_y(d):
         return {"par": (lax.rem(y + d, NY) * 2 + x_hi) * 2 + core}
 
+    def chip_at(offset):
+        return lax.rem(y + offset[0], NY) * 2 + lax.rem(x_hi + offset[1], 2)
+
+    def at_chip(to):
+        return {"par": to * 2 + core}
+
     other_core = {"par": chip * 2 + 1 - core}
     other_x = {"par": (y * 2 + 1 - x_hi) * 2 + core}
 
@@ -101,7 +110,7 @@
         return carry
 
     lax.fori_loop(1, NS, greet, 0)
-    in_plane = [other_core, other_x] + [along_y(d) for d in range(1, NY)]
+    in_plane = [other_core] + [at_chip(chip_at(offset)) for offset in CHIP_OFFSETS]
     for device in in_plane:
         pl.semaphore_signal(barrier, inc=1, device_id=device, device_id_type=MESH)
 
@@ -143,18 +152,32 @@
     own[chunk(me), :] = sorted_rows[chunk(me), :]
     to_table.wait()
 
+    above = lax.rem(z + 1, NZ) * 2 + x
+    below = lax.rem(z + NZ - 1, NZ) * 2 + x
+    across = z * 2 + 1 - x
+    def hand_on_chunk(s):
+        for slot, to in ((1, above), (0, below), (2, across)):
+            landing = near[0].at[slot, chunk(s)]
+            remote(own.at[chunk(s)], landing, near_send.at[s // 2], near_recv.at[0, slot], {"samp": to}).start()
+
+    @pl.when(me < 2 * EARLY)
+    def _():
+        hand_on_chunk(me)
+
     def arrive(k, carry):
         s = lax.rem(me + NS - ring(k), NS)
         await_bytes(own.at[chunk(s)], rows_recv.at[k])
+
+        @pl.when(s < 2 * EARLY)
+        def _():
+            hand_on_chunk(s)
+
         return carry
 
     lax.fori_loop(1, NS, arrive, 0)
 
-    above = lax.rem(z + 1, NZ) * 2 + x
-    below = lax.rem(z + NZ - 1, NZ) * 2 + x
-    across = z * 2 + 1 - x
     step_rows = rows // STEPS
-    handed = [0]
+    handed = [EARLY]
 
     def hand_on(upto):
         for i in range(handed[0], upto):
@@ -177,11 +200,18 @@
     def to_ys(u):
         await_bytes(pair_in[u], pair_recv.at[u])
         shares[u][...] = parts[u][core] + pair_in[u][...]
-        for d in (1, 3, 2):
+        if u in DIRECT:
+            for i, offset in enumerate(CHIP_OFFSETS):
+                to = chip_at(offset)
+                remote(shares[u].at[to], y_in[u].at[i], send.at[units + u], chip_recv.at[u, i], at_chip(to)).start()
+            return
+        for d in (2, 1, 3):
             to = pl.ds(2 * lax.rem(y + d, NY), 2)
             remote(shares[u].at[to], y_in[u].at[d - 1], send.at[units + u], y_recv.at[u, d - 1], along_y(d)).start()
 
     def to_x(u):
+        if u in DIRECT:
+            return
         total = shares[u][pl.ds(2 * y, 2)]
         for i in range(NY - 1):
             await_bytes(y_in[u].at[i], y_recv.at[u, i])
@@ -189,7 +219,30 @@
         halves[u][...] = total
         remote(halves[u].at[1 - x_hi], x_in[u], send.at[2 * units + u], x_recv.at[u], other_x).start()
 
+    def to_x(u):
+        if u in DIRECT:
+            return
+        total = shares[u][pl.ds(2 * y, 2)]
+        for i in range(NY - 1):
+            await_bytes(y_in[u].at[i], y_recv.at[u, i])
+            total += y_in[u][i]
+        halves[u][...] = total
+        remote(halves[u].at[1 - x_hi], x_in[u], send.at[2 * units + u], x_recv.at[u], other_x).start()
+
+    def to_chips(u):
+        await_bytes(pair_in[u], pair_recv.at[u])
+        shares[u][...] = parts[u][core] + pair_in[u][...]
+        for i, offset in enumerate(CHIP_OFFSETS):
+            to = chip_at(offset)
+            remote(shares[u].at[to], y_in[u].at[i], send.at[units + u], chip_recv.at[u, i], at_chip(to)).start()
+
     def whole(u):
+        if u in DIRECT:
+            total = shares[u][chip]
+            for i in range(len(CHIP_OFFSETS)):
+                await_bytes(y_in[u].at[i], chip_recv.at[u, i])
+                total += y_in[u][i]
+            return total * scale
         await_bytes(x_in[u], x_recv.at[u])
         return (halves[u][x_hi] + x_in[u][...]) * scale
 
@@ -224,7 +277,7 @@
     def await_exchange(ref, sem):
         await_bytes(ref.at[pl.ds(0, NS - 1)], sem)
 
-    sent_mid, sent_home = 3 * units, 3 * units + 2
+    sent_mid, sent_home = 3 * units, 3 * units + 3
 
     def to_mid(n):
         exchange(piece[n], mid[n], send.at[sent_mid + n], mid_recv.at[n])
@@ -237,21 +290,20 @@
 
     def own_pieces():
         total = whole(0)
-        for i in range(16):
-            a, l = 8 * (i // 4), 128 * (i % 4)
-            piece[0][i] = total[a : a + 8, l : l + 128]
+        for i in range(NS):
+            a, l = 4 * (i // 4), 128 * (i % 4)
+            piece[0][i] = total[a : a + 4, l : l + 128]
 
     def first_pieces():
         total = whole(1)
-        for i in range(16):
-            r, a, l = i // 8, 8 * (i % 8 // 2), 128 * (i % 2)
-            piece[0][16 + i] = total[r, a : a + 8, l : l + 128]
-
-    def later_pieces(h):
-        total = whole(2 + h)
+        for i in range(NS):
+            r, a, l = i // 16, 4 * (i % 16 // 2), 128 * (i % 2)
+            piece[1][i] = total[r, a : a + 4, l : l + 128]
+
+    def later_pieces(h, total):
         for i in range(16):
             r, a = i // 8, 4 * (i % 8)
-            piece[1][16 * h + i] = total[r, a : a + 4]
+            piece[2][16 * h + i] = total[r, a : a + 4]
 
     hand_on(WINDOW)
     own_tile(0)
@@ -265,30 +317,33 @@
     to_ys(1)
     hand_on(STEPS)
     own_pieces()
+    to_mid(0)
     partner_tiles(2, 1)
     to_ys(2)
+    partner_tiles(3, 2)
     to_x(1)
-    partner_tiles(3, 2)
+    to_ys(3)
     to_x(2)
-    to_ys(3)
+    to_home(0)
     first_pieces()
-    to_mid(0)
-    later_pieces(0)
-    to_x(3)
-    later_pieces(1)
     to_mid(1)
-    to_home(0)
+    later_pieces(0, whole(2))
+    later_pieces(1, whole(3))
+    to_mid(2)
+    await_exchange(home[0], home_recv.at[0])
+    for i in range(NS):
+        a, l = 4 * (i // 4), 128 * (i % 4)
+        out[0, a : a + 4, l : l + 128] = home[0][i]
     to_home(1)
-    await_exchange(home[0], home_recv.at[0])
-    for i in range(16):
-        a, l = 8 * (i // 4), 128 * (i % 4)
-        out[0, a : a + 8, l : l + 128] = home[0][i]
-        r, a, l = i // 8, 8 * (i % 8 // 2), 128 * (i % 2)
-        out[1 + r, a : a + 8, l : l + 128] = home[0][16 + i]
+    to_home(2)
     await_exchange(home[1], home_recv.at[1])
     for i in range(NS):
+        r, a, l = i // 16, 4 * (i % 16 // 2), 128 * (i % 2)
+        out[1 + r, a : a + 4, l : l + 128] = home[1][i]
+    await_exchange(home[2], home_recv.at[2])
+    for i in range(NS):
         h, r, a = i // 16, i % 16 // 8, 4 * (i % 8)
-        out[1 + r, a : a + 4, 256 + 128 * h : 384 + 128 * h] = home[1][i]
+        out[1 + r, a : a + 4, 256 + 128 * h : 384 + 128 * h] = home[2][i]
 
     await_bytes(own.at[pl.ds(0, rows - per)], rows_send)
     for i in range(STEPS - WINDOW, STEPS):
@@ -296,8 +351,9 @@
     for u in range(units):
         await_bytes(pair_in[u], send.at[u])
         await_bytes(y_in[u], send.at[units + u])
-        await_bytes(x_in[u], send.at[2 * units + u])
-    for n in range(2):
+        if u not in DIRECT:
+            await_bytes(x_in[u], send.at[2 * units + u])
+    for n in range(3):
         await_exchange(piece[n], send.at[sent_mid + n])
         await_exchange(turned[n], send.at[sent_home + n])
 
@@ -305,11 +361,11 @@
 def shards(logder, block_of, plan):
     rows, columns = logder.shape
     share = rows // (2 * CHIPS)
-    anywhere = pl.BlockSpec(memory_space=pl.ANY)
+    hbm = pl.BlockSpec(memory_space=pltpu.HBM)
     scale = 1.0 / math.sqrt(columns * lax.axis_size("par"))
     f32, bf16, i32 = jnp.float32, jnp.bfloat16, jnp.int32
     kinds = ((share, rows),) + tuple((2, share, count) for _, count in GROUPS)
-    sizes = (8, 4)
+    sizes = (4, 4, 4)
 
     def buffers(*lead):
         return [pltpu.VMEM(lead + kind, f32) for kind in kinds]
@@ -323,7 +379,7 @@
         functools.partial(tiles_kernel, scale),
         name="tiles",
         out_shape=jax.ShapeDtypeStruct((3, share, rows), f32),
-        in_specs=[anywhere, anywhere, anywhere],
+        in_specs=[hbm, hbm, hbm],
         out_specs=pl.BlockSpec(memory_space=pltpu.VMEM),
         scratch_shapes=[
             pltpu.VMEM((rows, columns), bf16),
@@ -337,7 +393,7 @@
             buffers(2, CHIPS),
             buffers(CHIPS),
             buffers(CHIPS),
-            buffers(NY - 1, 2),
+            [pltpu.VMEM(((CHIPS - 1,) if u in DIRECT else (NY - 1, 2)) + kind, f32) for u, kind in enumerate(kinds)],
             buffers(2),
             buffers(),
             pieces(),
@@ -353,6 +409,7 @@
             sems((units,)),
             sems((units, NY - 1)),
             sems((units,)),
+            sems((units, CHIPS - 1)),
             sems((len(sizes),)),
             sems((len(sizes),)),
         ],

time: 120 us -> 118 us (0.983)
  Pallas kernels: 118 us -> 116 us
    pallas_call x1, Pallas kernels: 118 us -> 116 us  [shards(): pl.pallas_call(functools.partial(tiles_kernel, scale), name='tiles', out_...]
where the time goes in v3:
time: 118 us
  Pallas kernels  116 us (98%)
  local copies, waits for them, and re-layouts  1.62 us (1%)
    pallas_call x1, Pallas kernels, shards(): pl.pallas_call(functools.partial(tiles_kernel, scale), name='tiles', out_...  116 us

profile of v3, /device:TPU:1, one launch (start us, length us, event | category | flops | bytes accessed | tf_op | source)
XLA Modules:
  0.0 117.7 jit_solution(8327689978272096393)
XLA Ops:
  0.0 116.0 %tiles.1 = f32[3,32,512]{2,1,0:T(8,128)} custom-call(bf16[512,1024]{1,0:T(8,128)(2,1)} %logder.1, s32[1,512]{1,0:T(1,128)} %bitcast.1, s32[2,32]{1,0:T(2,128)} %plan.1), custom_call_target="tpu_custom_call" | custom-call | tf_op jit(solution)/shard_map/tiles/pallas_call | solution.py:378
  116.0 1.6 %copy.5 = f32[3,32,512]{2,1,0:T(8,128)} copy(f32[3,32,512]{2,1,0:T(8,128)} %tiles.1) | data formatting | bytes 393216

commit v4 on v3

--- a/solution.py
+++ b/solution.py
@@ -18,7 +18,7 @@
 STEPS = 16
 WINDOW = 8
 DIRECT = (3,)
-EARLY = 2
+EARLY = 4
 BITS = (-0x55555556, -0x33333334, -0x0F0F0F10, -0x00FF0100, -0x00010000)
 
 
@@ -165,8 +165,8 @@
         hand_on_chunk(me)
 
     def arrive(k, carry):
-        s = lax.rem(me + NS - ring(k), NS)
-        await_bytes(own.at[chunk(s)], rows_recv.at[k])
+        s = lax.rem(me + NS - ring(NS - k), NS)
+        await_bytes(own.at[chunk(s)], rows_recv.at[NS - k])
 
         @pl.when(s < 2 * EARLY)
         def _():

time: 118 us -> 116 us (0.983)
  Pallas kernels: 116 us -> 114 us
    pallas_call x1, Pallas kernels: 116 us -> 114 us  [shards(): pl.pallas_call(functools.partial(tiles_kernel, scale), name='tiles', out_...]
where the time goes in v4:
time: 116 us
  Pallas kernels  114 us (98%)
  local copies, waits for them, and re-layouts  1.62 us (1%)
    pallas_call x1, Pallas kernels, shards(): pl.pallas_call(functools.partial(tiles_kernel, scale), name='tiles', out_...  114 us

profile of v4, /device:TPU:1, one launch (start us, length us, event | category | flops | bytes accessed | tf_op | source)
XLA Modules:
  0.0 115.6 jit_solution(10147573459122567152)
XLA Ops:
  0.0 113.9 %tiles.1 = f32[3,32,512]{2,1,0:T(8,128)} custom-call(bf16[512,1024]{1,0:T(8,128)(2,1)} %logder.1, s32[1,512]{1,0:T(1,128)} %bitcast.1, s32[2,32]{1,0:T(2,128)} %plan.1), custom_call_target="tpu_custom_call" | custom-call | tf_op jit(solution)/shard_map/tiles/pallas_call | solution.py:378
  113.9 1.6 %copy.5 = f32[3,32,512]{2,1,0:T(8,128)} copy(f32[3,32,512]{2,1,0:T(8,128)} %tiles.1) | data formatting | bytes 393216
